TPU v7x, 32 devices: a whole 2x2x4 slice. The times are simulated.
32 devices in a mesh: block: 8 (over z, x), tok: 4 (over y, core).
Axes of the slice: x: 2, y: 2, z: 4, core: 2. Of those that a mesh axis runs over, the one named last changes fastest.
Arguments:
- fast_in: float32 [8, 4, 3, 512, 512], P('block', 'tok'), may hold values from -0.25 to 0.25
- queries: bfloat16 [3, 8, 512, 2048], P(None, 'block', 'tok'), may hold values from -6 to 6
- keys: bfloat16 [3, 8, 512, 2048], P(None, 'block', 'tok'), may hold values from -6 to 6
- values: bfloat16 [3, 8, 512, 2048], P(None, 'block', 'tok'), may hold values from -6 to 6
- rates: bfloat16 [3, 8, 512, 4], P(None, 'block', 'tok'), may hold values from 0.0009765625 to 0.0078125
Outputs:
- outputs: bfloat16 [3, 8, 512, 2048], P(None, 'block', 'tok')
- fast_out: float32 [8, 4, 3, 512, 512], P('block', 'tok')
All inputs are finite; a program needn't handle non-finite values.
Results may differ from a plain program's by a relative error of at most 0.002.
Values may be sent and summed in bfloat16 or wider, within the bound.
A program may use at most 128 MiB of HBM per device.

v0:
```python
import functools
import math

import jax
import jax.numpy as jnp
from jax import lax
from jax.experimental import pallas as pl
from jax.experimental.pallas import tpu as pltpu
from jax.sharding import PartitionSpec as P

MESH = pl.DeviceIdType.MESH
epsilon = 1e-06
BF, F32 = jnp.bfloat16, jnp.float32
CHUNK = 256


def mm(a, b, dims=((1,), (0,))):
    return lax.dot_general(a, b, (dims, ((), ())), preferred_element_type=F32)


def split(x):
    hi = x.astype(BF)
    return hi, (x - hi.astype(F32)).astype(BF)


def encode(x):
    two = x * x
    return (two * two * two * x * jnp.abs(x)).astype(BF)


def decode(y):
    y = y.astype(F32)
    root = lax.rsqrt(lax.rsqrt(lax.rsqrt(jnp.maximum(jnp.abs(y), 2.0 ** -126))))
    two = root * root
    return y * (two * two * two * root)


def kernel(blocks, toks, scale, fast_ref, q_ref, k_ref, v_ref, rate_ref, out_ref, fast_out_ref,
           held, rate_wide, wf, whi, wlo, wsend, wrecv, abuf, xbuf, obuf, eta,
           recv_sem, send_sem, wload_sem, wsend_sem, wrecv_sem, orecv_sem, osend_sem):
    steps = q_ref.shape[0]
    part = q_ref.shape[2]
    width = wf.shape[1]
    length = held.shape[2]
    rows_of = min(CHUNK, width, length)
    b, t = lax.axis_index("block"), lax.axis_index("tok")
    after, before = lax.rem(b + 1, blocks), lax.rem(b + blocks - 1, blocks)
    after2, before2 = lax.rem(b + 2, blocks), lax.rem(b + blocks - 2, blocks)
    near = lax.div(t, 2) * 2
    mate = near + lax.rem(t + 1, 2)
    far = [lax.rem(near + 2 + j, toks) for j in range(2)]
    others = far + [mate]
    sources = (k_ref, v_ref, q_ref)

    def load_w(m):
        return pltpu.make_async_copy(fast_ref.at[0, 0, m], wf.at[m], wload_sem.at[m])

    for m in range(3):
        load_w(m).start()

    def src_of(s, a, dest):
        if a == 3:
            return rate_wide.at[s, dest]
        return sources[a].at[s, 0, :, pl.ds(pl.multiple_of(dest * width, width), width)]

    def dst_of(s, a, origin):
        rows = pl.ds(pl.multiple_of(origin * part, part), part)
        return eta.at[s, rows] if a == 3 else held.at[a, s, rows]

    def own(s, a):
        return pltpu.make_async_copy(src_of(s, a, t), dst_of(s, a, t), recv_sem.at[s, a, t])

    sends = []

    def send(s, a, block, dest, slot):
        copy = pltpu.make_async_remote_copy(
            src_ref=src_of(s, a, dest), dst_ref=dst_of(s, a, t),
            send_sem=send_sem.at[s, a, slot], recv_sem=recv_sem.at[s, a, t],
            device_id=(block, dest), device_id_type=MESH)
        copy.start()
        sends.append(copy)

    def exchange(s, a):
        for slot, dest in enumerate(others):
            send(s, a, b, dest, slot)

    def wait_tokens(s, a):
        for origin in range(toks):
            ref = dst_of(s, a, origin)
            pltpu.make_async_copy(ref, ref, recv_sem.at[s, a, origin]).wait()

    for a in (0, 1, 2):
        own(0, a).start()
        own(2, a).start()
    for s in range(steps):
        for h in range(toks):
            rate_wide[s, h] = jnp.broadcast_to(rate_ref[s, 0, :, h:h + 1], rate_wide.shape[2:])
    own(0, 3).start()
    own(2, 3).start()

    barrier = pltpu.get_barrier_semaphore()
    greet = [(b, dest) for dest in others]
    greet += [(block, tok) for block in (after, before) for tok in range(toks)]
    greet += [(after2, t), (before2, t)]
    for device in greet:
        pl.semaphore_signal(barrier, inc=1, device_id=device, device_id_type=MESH)
    pl.semaphore_wait(barrier, len(greet))

    for a in (0, 3, 1):
        exchange(0, a)
    for a in (0, 3, 1):
        for slot, dest in enumerate((near, near + 1)):
            send(1, a, after, dest, 2 + slot)

    def split_weights(m):
        @pl.loop(0, width // rows_of)
        def _(i):
            rows = pl.ds(pl.multiple_of(i * rows_of, rows_of), rows_of)
            whi[m, rows], wlo[m, rows] = split(wf[m, rows])

    for m in range(3):
        load_w(m).wait()
        split_weights(m)

    def forward(s):
        @pl.loop(0, length // rows_of)
        def _(i):
            rows = pl.ds(pl.multiple_of(i * rows_of, rows_of), rows_of)
            k, v = held[0, s, rows], held[1, s, rows]
            rate = eta[s, rows].astype(F32)
            rate = jnp.concatenate([rate] * (width // rate.shape[1]), axis=1)
            hidden = mm(k, whi[0]) + mm(k, wlo[0])
            gated = mm(k, whi[1]) + mm(k, wlo[1])
            gate_sig = jax.nn.sigmoid(hidden)
            active = hidden * gate_sig
            abuf[0, rows], abuf[1, rows] = split(rate * (active * gated))
            back = rate * (mm(v, whi[2], ((1,), (1,))) + mm(v, wlo[2], ((1,), (1,))))
            first = back * gated * gate_sig * (1.0 + hidden * (1.0 - gate_sig))
            xbuf[0, rows], xbuf[1, rows] = split(first)
            xbuf[2, rows], xbuf[3, rows] = split(back * active)

    def update(s, m, passing):
        @pl.loop(0, width // rows_of)
        def _(i):
            at = pl.multiple_of(i * rows_of, rows_of)
            rows = pl.ds(at, rows_of)
            over = ((0,), (0,))
            if m == 2:
                v = held[1, s]
                grad = mm(abuf[0, :, rows], v, over) + mm(abuf[1, :, rows], v, over)
            else:
                k = held[0, s, :, rows]
                grad = mm(k, xbuf[2 * m], over) + mm(k, xbuf[2 * m + 1], over)
            old = wf[m, rows]
            new = old + grad
            rescale = jnp.sqrt((jnp.mean(old * old, axis=1, keepdims=True) + epsilon)
                               / (jnp.mean(new * new, axis=1, keepdims=True) + epsilon))
            new = new * rescale
            wf[m, rows] = new
            whi[m, rows], wlo[m, rows] = split(new)
            if passing:
                wsend[m, rows] = encode(new * scale)

    def apply(s):
        @pl.loop(0, length // rows_of)
        def _(i):
            rows = pl.ds(pl.multiple_of(i * rows_of, rows_of), rows_of)
            q = held[2, s, rows]
            hidden = mm(q, whi[0]) + mm(q, wlo[0])
            gated = mm(q, whi[1]) + mm(q, wlo[1])
            hi, lo = split(jax.nn.silu(hidden) * gated)
            result = mm(hi, whi[2]) + (mm(lo, whi[2]) + mm(hi, wlo[2]))
            obuf[s, rows] = result.astype(BF)

    def out_at(s, origin):
        return out_ref.at[s, 0, :, pl.ds(pl.multiple_of(origin * width, width), width)]

    def out_part(s, dest):
        return obuf.at[s, pl.ds(pl.multiple_of(dest * part, part), part)]

    def send_out(s, block, dests):
        for slot, dest in enumerate(dests):
            copy = pltpu.make_async_remote_copy(
                src_ref=out_part(s, dest), dst_ref=out_at(s, t),
                send_sem=osend_sem.at[s, slot], recv_sem=orecv_sem.at[s, t],
                device_id=(block, dest), device_id_type=MESH)
            copy.start()
            sends.append(copy)

    def own_out(s):
        pltpu.make_async_copy(out_part(s, t), out_at(s, t), orecv_sem.at[s, t]).start()

    def hand_on(m):
        return pltpu.make_async_remote_copy(
            src_ref=wsend.at[m], dst_ref=wrecv.at[m], send_sem=wsend_sem.at[m],
            recv_sem=wrecv_sem.at[m], device_id=(after2, t), device_id_type=MESH)

    for a in (0, 3, 1):
        wait_tokens(0, a)
    for a in (0, 3, 1):
        for slot, dest in enumerate(far):
            send(1, a, after, dest, slot)
    forward(0)
    for m in (2, 0, 1):
        update(0, m, True)
        hand_on(m).start()
    exchange(0, 2)
    for a in (0, 3, 1, 2):
        exchange(2, a)
    wait_tokens(0, 2)
    apply(0)
    send_out(0, b, others)
    own_out(0)

    for m in (2, 0, 1):
        hand_on(m).wait()
        if m == 1:
            for slot, dest in enumerate(far + [near, near + 1]):
                send(1, 2, after, dest, slot)

        @pl.loop(0, width // rows_of)
        def _(i):
            rows = pl.ds(pl.multiple_of(i * rows_of, rows_of), rows_of)
            fresh = decode(wrecv[m, rows]) * (1.0 / scale)
            wf[m, rows] = fresh
            whi[m, rows], wlo[m, rows] = split(fresh)
    for a in (0, 3, 1):
        wait_tokens(1, a)
    forward(1)
    for m in (2, 0, 1):
        update(1, m, False)
    wait_tokens(1, 2)
    apply(1)
    send_out(1, before, far + [near, near + 1])

    for a in (0, 3, 1):
        wait_tokens(2, a)
    forward(2)
    for m in (2, 0, 1):
        update(2, m, False)
        pltpu.make_async_copy(wf.at[m], fast_out_ref.at[0, 0, m], wload_sem.at[m]).start()
    wait_tokens(2, 2)
    apply(2)
    send_out(2, b, others)
    own_out(2)

    for s in range(steps):
        for origin in range(toks):
            ref = out_at(s, origin)
            pltpu.make_async_copy(ref, ref, orecv_sem.at[s, origin]).wait()
    for m in range(3):
        pltpu.make_async_copy(wf.at[m], fast_out_ref.at[0, 0, m], wload_sem.at[m]).wait()
    for copy in sends:
        copy.wait_send()


def local(fast_in, queries, keys, values, rates):
    blocks, toks = lax.axis_size("block"), lax.axis_size("tok")
    steps, _, part, _ = queries.shape
    width = fast_in.shape[-1]
    length = part * toks
    scale = 2.0 ** math.floor(math.log2(2.0 ** 15.8 / (0.2501 * math.sqrt(width))))
    anywhere = pl.BlockSpec(memory_space=pl.ANY)
    vmem, dma = pltpu.VMEM, pltpu.SemaphoreType.DMA
    lanes = 128
    return pl.pallas_call(
        functools.partial(kernel, blocks, toks, scale),
        out_shape=(jax.ShapeDtypeStruct(queries.shape, queries.dtype),
                   jax.ShapeDtypeStruct(fast_in.shape, fast_in.dtype)),
        in_specs=[anywhere] * 4 + [pl.BlockSpec(memory_space=pltpu.VMEM)],
        out_specs=(anywhere, anywhere),
        scratch_shapes=[
            vmem((3, steps, length, width), BF),
            vmem((steps, toks, part, lanes), BF),
            vmem((3, width, width), F32),
            vmem((3, width, width), BF),
            vmem((3, width, width), BF),
            vmem((3, width, width), BF),
            vmem((3, width, width), BF),
            vmem((2, length, width), BF),
            vmem((4, length, width), BF),
            vmem((steps, length, width), BF),
            vmem((steps, length, lanes), BF),
            dma((steps, 4, toks)), dma((steps, 4, toks)),
            dma((3,)), dma((3,)), dma((3,)),
            dma((steps, toks)), dma((steps, toks)),
        ],
        compiler_params=pltpu.CompilerParams(
            collective_id=0, has_side_effects=True, vmem_limit_bytes=48 * 2**20),
        cost_estimate=pl.CostEstimate(
            flops=57 * 2 * length * width * width, bytes_accessed=2**24, transcendentals=0),
    )(fast_in, queries, keys, values, rates)


def solution(mesh):
    tokens = P(None, "block", "tok", None)
    weights = P("block", "tok", None, None, None)
    return jax.shard_map(
        local, mesh=mesh, in_specs=(weights, tokens, tokens, tokens, tokens),
        out_specs=(tokens, weights), check_vma=False)
```

profile of v0, /device:TPU:1, one launch (start us, length us, event | category | flops | bytes accessed | tf_op | source)
XLA Modules:
  0.0 107.3 jit_solution(4731269250113491559)
XLA Ops:
  0.6 0.9 copy.7.rate_ref
  1.5 0.0 copy-start
  1.5 1.4 %copy-done = bf16[3,1,128,2048]{3,2,1,0:T(8,128)(2,1)S(1)} copy-done((bf16[3,1,128,2048]{3,2,1,0:T(8,128)(2,1)S(1)}, bf16[3,1,128,2048]{3,2,1,0:T(8,128)(2,1)}, u32[]{:S(2)}) %copy-start) | copy-done | bytes 1572888
  2.9 0.0 copy-start.1
  2.9 1.4 %copy-done.1 = bf16[3,1,128,2048]{3,2,1,0:T(8,128)(2,1)S(1)} copy-done((bf16[3,1,128,2048]{3,2,1,0:T(8,128)(2,1)S(1)}, bf16[3,1,128,2048]{3,2,1,0:T(8,128)(2,1)}, u32[]{:S(2)}) %copy-start.1) | copy-done | bytes 1572888
  4.3 98.8 %shard_map.68 = (bf16[3,1,128,2048]{3,2,1,0:T(8,128)(2,1)S(1)}, f32[1,1,3,512,512]{4,3,2,1,0:T(8,128)}) custom-call(f32[1,1,3,512,512]{4,3,2,1,0:T(8,128)} %fast_ref.1, bf16[3,1,128,2048]{3,2,1,0:T(8,128)(2,1)S(1)} %copy-done, bf16[3,1,128,2048]{3,2,1,0:T(8,128)(2,1)S(1)} %copy-done.1, bf16[3,1,128,2048]{3,2,1,0:T(8,128)(2,1)} %v_ref.1, ...), custom_call_target="tpu_custom_call" | custom-call | flops 15300820992 | bytes 16777216 | tf_op jit(solution)/shard_map/pallas_call | solution.py:266
  103.2 0.0 copy-start.2
  103.2 1.1 %copy.10 = bf16[3,1,128,2048]{3,2,1,0:T(8,128)(2,1)} copy(bf16[3,1,128,2048]{3,2,1,0:T(8,128)(2,1)S(1)} %get-tuple-element.4) | data formatting | bytes 3145728
  104.3 1.3 %copy-done.2 = f32[1,1,3,512,512]{4,3,2,1,0:T(8,128)S(1)} copy-done((f32[1,1,3,512,512]{4,3,2,1,0:T(8,128)S(1)}, f32[1,1,3,512,512]{4,3,2,1,0:T(8,128)}, u32[]{:S(2)}) %copy-start.2) | copy-done | bytes 3145752
  105.6 1.7 %copy.11 = f32[1,1,3,512,512]{4,3,2,1,0:T(8,128)} copy(f32[1,1,3,512,512]{4,3,2,1,0:T(8,128)S(1)} %copy-done.2) | data formatting | bytes 6291456
Async XLA Ops:
  1.5 1.4 %copy-start = (bf16[3,1,128,2048]{3,2,1,0:T(8,128)(2,1)S(1)}, bf16[3,1,128,2048]{3,2,1,0:T(8,128)(2,1)}, u32[]{:S(2)}) copy-start(bf16[3,1,128,2048]{3,2,1,0:T(8,128)(2,1)} %q_ref.1) | copy-start | bytes 4718596
  2.9 1.4 %copy-start.1 = (bf16[3,1,128,2048]{3,2,1,0:T(8,128)(2,1)S(1)}, bf16[3,1,128,2048]{3,2,1,0:T(8,128)(2,1)}, u32[]{:S(2)}) copy-start(bf16[3,1,128,2048]{3,2,1,0:T(8,128)(2,1)} %k_ref.1) | copy-start | bytes 4718596
  103.2 2.5 %copy-start.2 = (f32[1,1,3,512,512]{4,3,2,1,0:T(8,128)S(1)}, f32[1,1,3,512,512]{4,3,2,1,0:T(8,128)}, u32[]{:S(2)}) copy-start(f32[1,1,3,512,512]{4,3,2,1,0:T(8,128)} %get-tuple-element.5) | copy-start | bytes 9437188
where the time goes:
time: 108 us; the launch traced here: 107 us
  Pallas kernels  98.8 us (91%)
  local copies, waits for them, and re-layouts  7.79 us (7%)
    pallas_call x1, Pallas kernels, local(): pl.pallas_call(functools.partial(kernel, blocks, toks, scale), out_shape=...  98.8 us
    unnamed x9, local copies, waits for them, and re-layouts  7.79 us

commit v1 on v0

v1 whole, which is shorter than its diff:
```python
import functools
import math

import jax
import jax.numpy as jnp
from jax import lax
from jax.experimental import pallas as pl
from jax.experimental.pallas import tpu as pltpu
from jax.sharding import PartitionSpec as P

MESH = pl.DeviceIdType.MESH
epsilon = 1e-06
BF, F32 = jnp.bfloat16, jnp.float32
CHUNK = 256


def mm(a, b, dims=((1,), (0,))):
    return lax.dot_general(a, b, (dims, ((), ())), preferred_element_type=F32)


def split(x):
    hi = x.astype(BF)
    return hi, (x - hi.astype(F32)).astype(BF)


def encode(x):
    two = x * x
    return (two * two * two * x * jnp.abs(x)).astype(BF)


def decode(y):
    y = y.astype(F32)
    root = lax.rsqrt(lax.rsqrt(lax.rsqrt(jnp.maximum(jnp.abs(y), 2.0 ** -126))))
    two = root * root
    return y * (two * two * two * root)


def kernel(blocks, toks, scale, fast_ref, q_ref, k_ref, v_ref, rate_ref, out_ref, fast_out_ref,
           held, rate_wide, wf, whi, wlo, wsend, wrecv, abuf, fbuf, xbuf, obuf, eta,
           recv_sem, send_sem, wload_sem, wsend_sem, wrecv_sem, orecv_sem, osend_sem):
    steps = q_ref.shape[0]
    part = q_ref.shape[2]
    width = wf.shape[1]
    length = held.shape[2]
    rows_of = min(CHUNK, width, length)
    b, t = lax.axis_index("block"), lax.axis_index("tok")
    odd = lax.rem(b, 2)
    pair = b + 1 - 2 * odd
    after2, before2 = lax.rem(b + 2, blocks), lax.rem(b + blocks - 2, blocks)
    near = lax.div(t, 2) * 2
    mate = near + lax.rem(t + 1, 2)
    far = [lax.rem(near + 2 + j, toks) for j in range(2)]
    side = [near, near + 1]
    others = far + [mate]
    sources = (k_ref, v_ref, q_ref)
    K, V, Q, RATE = range(4)

    def load_w(m):
        return pltpu.make_async_copy(fast_ref.at[0, 0, m], wf.at[m], wload_sem.at[m])

    for m in range(3):
        load_w(m).start()

    def src_of(s, a, dest):
        if a == RATE:
            return rate_wide.at[s, dest]
        return sources[a].at[s, 0, :, pl.ds(pl.multiple_of(dest * width, width), width)]

    def dst_of(s, a, origin):
        rows = pl.ds(pl.multiple_of(origin * part, part), part)
        return eta.at[s, rows] if a == RATE else held.at[a, s, rows]

    def own(s, a):
        return pltpu.make_async_copy(src_of(s, a, t), dst_of(s, a, t), recv_sem.at[s, a, t])

    sends = []

    def send(s, a, block, dest, slot):
        copy = pltpu.make_async_remote_copy(
            src_ref=src_of(s, a, dest), dst_ref=dst_of(s, a, t),
            send_sem=send_sem.at[s, a, slot], recv_sem=recv_sem.at[s, a, t],
            device_id=(block, dest), device_id_type=MESH)
        copy.start()
        sends.append(copy)

    def exchange(s, a):
        for slot, dest in enumerate(others):
            send(s, a, b, dest, slot)

    def wait_tokens(s, *arrays):
        for a in arrays:
            for origin in range(toks):
                ref = dst_of(s, a, origin)
                pltpu.make_async_copy(ref, ref, recv_sem.at[s, a, origin]).wait()

    for a in (K, V, Q):
        own(0, a).start()
        own(2, a).start()
    for s in range(steps):
        for h in range(toks):
            rate_wide[s, h] = jnp.broadcast_to(rate_ref[s, 0, :, h:h + 1], rate_wide.shape[2:])
    own(0, RATE).start()
    own(2, RATE).start()

    barrier = pltpu.get_barrier_semaphore()
    greet = [(b, dest) for dest in others] + [(pair, tok) for tok in range(toks)]
    greet += [(after2, t), (before2, t)]
    for device in greet:
        pl.semaphore_signal(barrier, inc=1, device_id=device, device_id_type=MESH)
    pl.semaphore_wait(barrier, len(greet))

    for a in (K, RATE, V):
        exchange(0, a)
    for a in (K, RATE, V):
        for slot, dest in enumerate(side):
            send(1, a, pair, dest, 2 + slot)

    def each(count):
        return pl.loop(0, count // rows_of)

    def chunk(i):
        return pl.ds(pl.multiple_of(i * rows_of, rows_of), rows_of)

    for m in range(3):
        load_w(m).wait()

        @each(width)
        def _(i):
            rows = chunk(i)
            whi[0, m, rows], wlo[0, m, rows] = split(wf[m, rows])

    def forward(s, bank):
        @each(length)
        def _(i):
            rows = chunk(i)
            k = held[K, s, rows]
            rate = eta[s, rows].astype(F32)
            rate = jnp.concatenate([rate] * (width // rate.shape[1]), axis=1)
            hidden = mm(k, whi[bank, 0]) + mm(k, wlo[bank, 0])
            gated = mm(k, whi[bank, 1]) + mm(k, wlo[bank, 1])
            gate_sig = jax.nn.sigmoid(hidden)
            active = rate * (hidden * gate_sig)
            abuf[0, rows], abuf[1, rows] = split(active * gated)
            fbuf[0, rows] = rate * gated * gate_sig * (1.0 + hidden * (1.0 - gate_sig))
            fbuf[1, rows] = active

    def backward(s, bank):
        @each(length)
        def _(i):
            rows = chunk(i)
            v = held[V, s, rows]
            over = ((1,), (1,))
            back = mm(v, whi[bank, 2], over) + mm(v, wlo[bank, 2], over)
            xbuf[0, rows], xbuf[1, rows] = split(back * fbuf[0, rows])
            xbuf[2, rows], xbuf[3, rows] = split(back * fbuf[1, rows])

    def update(s, m, bank):
        @each(width)
        def _(i):
            rows = chunk(i)
            over = ((0,), (0,))
            if m == 2:
                v = held[V, s]
                grad = mm(abuf[0, :, rows], v, over) + mm(abuf[1, :, rows], v, over)
            else:
                k = held[K, s, :, rows]
                grad = mm(k, xbuf[2 * m], over) + mm(k, xbuf[2 * m + 1], over)
            old = wf[m, rows]
            new = old + grad
            rescale = jnp.sqrt((jnp.mean(old * old, axis=1, keepdims=True) + epsilon)
                               / (jnp.mean(new * new, axis=1, keepdims=True) + epsilon))
            new = new * rescale
            wf[m, rows] = new
            whi[bank, m, rows], wlo[bank, m, rows] = split(new)

    def hand_on(m):
        return pltpu.make_async_remote_copy(
            src_ref=wsend.at[m], dst_ref=wrecv.at[m], send_sem=wsend_sem.at[m],
            recv_sem=wrecv_sem.at[m], device_id=(after2, t), device_id_type=MESH)

    def give(m):
        @each(width)
        def _(i):
            rows = chunk(i)
            wsend[m, rows] = encode(wf[m, rows] * scale)

        hand_on(m).start()

    def take(m, bank):
        hand_on(m).wait_recv()

        @each(width)
        def _(i):
            rows = chunk(i)
            fresh = decode(wrecv[m, rows]) * (1.0 / scale)
            wf[m, rows] = fresh
            whi[bank, m, rows], wlo[bank, m, rows] = split(fresh)

    def out_at(s, origin):
        return out_ref.at[s, 0, :, pl.ds(pl.multiple_of(origin * width, width), width)]

    def out_part(s, dest):
        return obuf.at[s, pl.ds(pl.multiple_of(dest * part, part), part)]

    def out_copy(s, block, dest, slot):
        return pltpu.make_async_remote_copy(
            src_ref=out_part(s, dest), dst_ref=out_at(s, t),
            send_sem=osend_sem.at[s, slot], recv_sem=orecv_sem.at[s, t],
            device_id=(block, dest), device_id_type=MESH)

    def apply(s, bank):
        wait_tokens(s, Q)
        home = s != 1
        block = b if home else pair
        for turn, dests in enumerate((far, side)):
            rows = pl.ds(pl.multiple_of(dests[0] * part, 2 * part), 2 * part)
            q = held[Q, s, rows]
            hidden = mm(q, whi[bank, 0]) + mm(q, wlo[bank, 0])
            gated = mm(q, whi[bank, 1]) + mm(q, wlo[bank, 1])
            hi, lo = split(jax.nn.silu(hidden) * gated)
            result = mm(hi, whi[bank, 2]) + (mm(lo, whi[bank, 2]) + mm(hi, wlo[bank, 2]))
            obuf[s, rows] = result.astype(BF)
            if turn and home:
                dests = [mate]
                pltpu.make_async_copy(out_part(s, t), out_at(s, t), orecv_sem.at[s, t]).start()
            for slot, dest in enumerate(dests):
                out_copy(s, block, dest, 2 * turn + slot).start()

    def wait_out_sent(s):
        home = s != 1
        block = b if home else pair
        for slot, dest in enumerate(others if home else far + side):
            out_copy(s, block, dest, slot).wait_send()

    wait_tokens(0, K, RATE)
    forward(0, 0)
    wait_tokens(0, V)
    for a in (K, RATE, V):
        for slot, dest in enumerate(far):
            send(1, a, pair, dest, slot)
    backward(0, 0)
    for m in range(3):
        update(0, m, 1)

        @pl.when(odd == 1)
        def _():
            give(m)

    exchange(0, Q)
    for slot, dest in enumerate(far + side):
        send(1, Q, pair, dest, slot)
    for a in (K, RATE, V, Q):
        exchange(2, a)

    @pl.when(odd == 0)
    def _():
        wait_tokens(1, K, RATE)
        forward(1, 1)
        wait_tokens(1, V)
        backward(1, 1)
        for m in range(3):
            update(1, m, 3)
            give(m)

    apply(0, 1)

    @pl.when(odd == 0)
    def _():
        apply(1, 3)
        take(0, 2)
        take(1, 2)
        wait_tokens(2, K, RATE)
        forward(2, 2)
        take(2, 2)
        wait_tokens(2, V)
        backward(2, 2)

    @pl.when(odd == 1)
    def _():
        take(0, 2)
        take(1, 2)
        wait_tokens(1, K, RATE)
        forward(1, 2)
        take(2, 2)
        wait_tokens(1, V)
        backward(1, 2)
        for m in range(3):
            update(1, m, 3)
        apply(1, 3)
        wait_tokens(2, K, RATE)
        forward(2, 3)
        wait_tokens(2, V)
        backward(2, 3)

    for m in range(3):
        update(2, m, 0)
        pltpu.make_async_copy(wf.at[m], fast_out_ref.at[0, 0, m], wload_sem.at[m]).start()
    apply(2, 0)

    for s in range(steps):
        for origin in range(toks):
            ref = out_at(s, origin)
            pltpu.make_async_copy(ref, ref, orecv_sem.at[s, origin]).wait()
        wait_out_sent(s)
    for m in range(3):
        pltpu.make_async_copy(wf.at[m], fast_out_ref.at[0, 0, m], wload_sem.at[m]).wait()
        hand_on(m).wait_send()
    for copy in sends:
        copy.wait_send()


def local(fast_in, queries, keys, values, rates):
    blocks, toks = lax.axis_size("block"), lax.axis_size("tok")
    steps, _, part, _ = queries.shape
    width = fast_in.shape[-1]
    length = part * toks
    scale = 2.0 ** math.floor(math.log2(2.0 ** 15.8 / (0.2501 * math.sqrt(width))))
    anywhere = pl.BlockSpec(memory_space=pl.ANY)
    vmem, dma = pltpu.VMEM, pltpu.SemaphoreType.DMA
    lanes = 128
    return pl.pallas_call(
        functools.partial(kernel, blocks, toks, scale),
        out_shape=(jax.ShapeDtypeStruct(queries.shape, queries.dtype),
                   jax.ShapeDtypeStruct(fast_in.shape, fast_in.dtype)),
        in_specs=[anywhere] * 4 + [pl.BlockSpec(memory_space=pltpu.VMEM)],
        out_specs=(anywhere, anywhere),
        scratch_shapes=[
            vmem((3, steps, length, width), BF),
            vmem((steps, toks, part, lanes), BF),
            vmem((3, width, width), F32),
            vmem((4, 3, width, width), BF),
            vmem((4, 3, width, width), BF),
            vmem((3, width, width), BF),
            vmem((3, width, width), BF),
            vmem((2, length, width), BF),
            vmem((2, length, width), F32),
            vmem((4, length, width), BF),
            vmem((steps, length, width), BF),
            vmem((steps, length, lanes), BF),
            dma((steps, 4, toks)), dma((steps, 4, toks)),
            dma((3,)), dma((3,)), dma((3,)),
            dma((steps, toks)), dma((steps, toks)),
        ],
        compiler_params=pltpu.CompilerParams(
            collective_id=0, has_side_effects=True, vmem_limit_bytes=60 * 2**20),
        cost_estimate=pl.CostEstimate(
            flops=57 * 2 * length * width * width, bytes_accessed=2**24, transcendentals=0),
    )(fast_in, queries, keys, values, rates)


def solution(mesh):
    tokens = P(None, "block", "tok", None)
    weights = P("block", "tok", None, None, None)
    return jax.shard_map(
        local, mesh=mesh, in_specs=(weights, tokens, tokens, tokens, tokens),
        out_specs=(tokens, weights), check_vma=False)
```

time: 108 us -> 93.5 us (0.87)
  Pallas kernels: 98.8 us -> 86.6 us
  local copies, waits for them, and re-layouts: 7.79 us -> 6.02 us
    pallas_call x1, Pallas kernels: 98.8 us -> 86.6 us  [local(): pl.pallas_call(functools.partial(kernel, blocks, toks, scale), out_shape=...]
    unnamed x9 -> x5, local copies, waits for them, and re-layouts: 7.79 us -> 6.02 us
where the time goes in v1:
time: 93.5 us; the launch traced here: 93.3 us
  Pallas kernels  86.6 us (93%)
  local copies, waits for them, and re-layouts  6.02 us (6%)
    pallas_call x1, Pallas kernels, local(): pl.pallas_call(functools.partial(kernel, blocks, toks, scale), out_shape=...  86.6 us
    unnamed x5, local copies, waits for them, and re-layouts  6.02 us

profile of v1, /device:TPU:1, one launch (start us, length us, event | category | flops | bytes accessed | tf_op | source)
XLA Modules:
  0.0 93.3 jit_solution(13726162809236989281)
XLA Ops:
  0.6 1.5 %copy.7.rate_ref = bf16[3,1,128,4]{3,2,1,0:T(8,128)(2,1)} copy(bf16[3,1,128,4]{2,3,1,0:T(4,128)(2,1)} %param.9) | data formatting | bytes 6144 | tf_op args[4]
  2.1 86.6 %shard_map.68 = (bf16[3,1,128,2048]{3,2,1,0:T(8,128)(2,1)}, f32[1,1,3,512,512]{4,3,2,1,0:T(8,128)}) custom-call(f32[1,1,3,512,512]{4,3,2,1,0:T(8,128)} %fast_ref.1, bf16[3,1,128,2048]{3,2,1,0:T(8,128)(2,1)} %q_ref.1, bf16[3,1,128,2048]{3,2,1,0:T(8,128)(2,1)} %k_ref.1, bf16[3,1,128,2048]{3,2,1,0:T(8,128)(2,1)} %v_ref.1, bf16[3,1,128,4]{3,2,1,0:T(8,128)(2,1)} %copy.7.rate_ref), custom_call_target="tpu_custom_call" | custom-call | flops 15300820992 | bytes 16777216 | tf_op jit(solution)/shard_map/pallas_call | solution.py:321
  88.7 0.0 copy-start
  88.7 2.9 %copy.10 = bf16[3,1,128,2048]{3,2,1,0:T(8,128)(2,1)} copy(bf16[3,1,128,2048]{3,2,1,0:T(8,128)(2,1)} %get-tuple-element.4) | data formatting | bytes 3145728
  91.6 0.0 copy-done
  91.6 1.7 %copy.11 = f32[1,1,3,512,512]{4,3,2,1,0:T(8,128)} copy(f32[1,1,3,512,512]{4,3,2,1,0:T(8,128)S(1)} %copy-done) | data formatting | bytes 6291456
Async XLA Ops:
  88.7 2.9 %copy-start = (f32[1,1,3,512,512]{4,3,2,1,0:T(8,128)S(1)}, f32[1,1,3,512,512]{4,3,2,1,0:T(8,128)}, u32[]{:S(2)}) copy-start(f32[1,1,3,512,512]{4,3,2,1,0:T(8,128)} %get-tuple-element.5) | copy-start | bytes 9437188
